TPU v7x, 32 devices: a whole 2x2x4 slice. The times are simulated.
32 devices in a mesh: row: 4 (over z), col: 8 (over y, x, core).
Axes of the slice: x: 2, y: 2, z: 4, core: 2. Of those that a mesh axis runs over, the one named last changes fastest.
Arguments:
- trailing: float32 [16384, 16384], P('row', 'col'), as said below
- cross: float32 [1024, 16384], P(('row', 'col')), may hold values from -6 to 6
Outputs:
- factored: float32 [16384, 16384], P('row', 'col')
- solved: float32 [1024, 16384], P('row', 'col')
Inputs may be any that keep to these rules, and one draw needn't show every extreme that they name: trailing is symmetric and positive definite.
All inputs are finite; a program needn't handle non-finite values.
Results may differ from a plain program's by a relative error of at most 0.00025.
Values sent between devices are 32-bit elements; how exact they have to be, the bound alone decides.
A program may use at most 192 MiB of HBM per device.

v0:
```python
import jax
import jax.numpy as jnp
from jax import lax
from jax.sharding import PartitionSpec as P

B = 256


def from_root(shard, axis, root):
    mine = lax.axis_index(axis) == root
    return lax.psum(jnp.where(mine, shard, jnp.zeros_like(shard)), axis)


def on_device(trailing, cross):
    rows_count = lax.axis_size("row")
    cols_count = lax.axis_size("col")
    row_at = lax.axis_index("row")
    col_at = lax.axis_index("col")
    local_rows, local_cols = trailing.shape
    col_blocks = local_cols // B
    row_tile = jnp.arange(local_rows, dtype=jnp.int32) // B * rows_count + row_at
    col_tile = jnp.arange(local_cols, dtype=jnp.int32) // B * cols_count + col_at
    exact = lax.Precision.HIGHEST
    contract = (((1,), (1,)), ((), ()))
    ratio = cols_count // rows_count
    few_queries = cross.shape[0]
    spread = cross.reshape(few_queries, col_blocks, cols_count, B)
    moved = lax.all_to_all(spread, "col", split_axis=2, concat_axis=0, tiled=True)
    answer = moved.reshape(few_queries * cols_count, local_cols)

    def select_rows(source):
        shaped = source.reshape(col_blocks, ratio, B, B)
        chosen = lax.dynamic_index_in_dim(shaped, col_at // rows_count, axis=1, keepdims=False)
        return chosen.reshape(local_cols, B)

    def factorize(state, panel):
        home_row = panel % rows_count
        home_col = panel % cols_count
        row_block = panel // rows_count
        col_block = panel // cols_count
        slab = state[:, col_block * B : (col_block + 1) * B]
        corner = from_root(slab[row_block * B : (row_block + 1) * B], "row", home_row)
        factor = jnp.linalg.cholesky(corner)
        scaled = lax.linalg.triangular_solve(
            factor, slab, left_side=False, lower=True, transpose_a=True
        )
        below = jnp.where((row_tile > panel)[:, None], scaled, 0.0)
        column = jnp.where(
            (row_tile == panel)[:, None], jnp.tile(factor, (local_rows // B, 1)), below
        )
        across = from_root(column, "col", home_col)
        sent = from_root(across, "row", col_at % rows_count)
        mirror = select_rows(sent)
        return (factor, across, mirror)

    def update(state, pieces, first, last):
        start_col = first * B
        end_col = last * B
        lefts = [
            jnp.where((row_tile > panel)[:, None], across, 0.0) for across, mirror, panel in pieces
        ]
        rights = [
            jnp.where((col_tile > panel)[:, None], mirror, 0.0) for across, mirror, panel in pieces
        ]
        left_part = lefts[0]
        right_part = rights[0]
        change = lax.dot_general(
            left_part, right_part, contract, precision=exact, preferred_element_type=jnp.float32
        )
        return state.at[:, start_col:end_col].set(state - change)

    def finish(state, across, panel):
        home_row = panel % rows_count
        home_col = panel % cols_count
        row_block = panel // rows_count
        col_block = panel // cols_count
        block = state[:, col_block * B : (col_block + 1) * B]
        state = state.at[:, col_block * B : (col_block + 1) * B].set(
            jnp.where(col_at == home_col, across, block)
        )
        band = state[row_block * B : (row_block + 1) * B]
        wiped = jnp.logical_and(row_at == home_row, col_tile > panel)[None, :]
        return state.at[row_block * B : (row_block + 1) * B].set(jnp.where(wiped, 0.0, band))

    def forward(answer, factor, mirror, panel):
        home_col = panel % cols_count
        col_block = panel // cols_count
        target = answer[:, col_block * B : (col_block + 1) * B]
        result = lax.linalg.triangular_solve(
            factor, target, left_side=False, lower=True, transpose_a=True
        )
        shared = from_root(result, "col", home_col)
        masked = jnp.where((col_tile > panel)[:, None], mirror, 0.0)
        answer = answer - lax.dot_general(
            shared, masked, contract, precision=exact, preferred_element_type=jnp.float32
        )
        kept = answer[:, col_block * B : (col_block + 1) * B]
        return answer.at[:, col_block * B : (col_block + 1) * B].set(
            jnp.where(col_at == home_col, shared, kept)
        )

    state = trailing
    first_factor, first_across, first_mirror = factorize(state, 0)
    state = update(state, [(first_across, first_mirror, 0)], 0, col_blocks)
    state = finish(state, first_across, 0)
    second_factor, second_across, second_mirror = factorize(state, 1)
    state = update(state, [(second_across, second_mirror, 1)], 0, col_blocks)
    state = finish(state, second_across, 1)
    answer = forward(answer, first_factor, first_mirror, 0)
    answer = forward(answer, second_factor, second_mirror, 1)
    return (state, answer)


def solution(mesh):
    placed = (P("row", "col"), P(("row", "col"), None))
    return jax.shard_map(
        on_device,
        mesh=mesh,
        in_specs=placed,
        out_specs=(P("row", "col"), P("row", "col")),
        check_vma=False,
    )
```

profile of v0, /device:TPU:29, one launch (start us, length us, event | category | flops | bytes accessed | tf_op | source)
XLA Modules:
  0.0 944.0 jit_solution(9669560383149999181)
XLA Ops:
  7.2 31.2 %copy.20 = f32[4096,2048]{0,1:T(8,128)} copy(f32[4096,2048]{1,0:T(8,128)} %param.27) | data formatting | bytes 67108864 | tf_op args[0]
  47.8 26.4 %all-reduce.10.cloned.1.call-done = f32[256,256]{0,1:T(8,128)} async-done(((f32[256,256]{0,1:T(8,128)}), f32[256,256]{0,1:T(8,128)}) %all-reduce.10.cloned.1.call-update) | async-done | bytes 262160 | tf_op jit(solution)/shard_map/psum | solution.py:11
  76.3 11.7 %cholesky.130 = f32[128,128]{1,0:T(8,128)S(1)} custom-call(f32[128,128]{1,0:T(8,128)S(1)} %cholesky.194), custom_call_target="Cholesky" | custom-call | tf_op jit(solution)/shard_map/jit(cholesky)/cholesky | solution.py:43
  88.1 9.8 %custom-call.17 = f32[1,128,128]{1,2,0:T(8,128)S(1)} custom-call(f32[1,128,128]{2,1,0:T(8,128)S(1)} %get-tuple-element.192), custom_call_target="InvertDiagBlocksLowerTriangular" | custom-call | tf_op jit(solution)/shard_map/jit(cholesky)/cholesky | solution.py:43
  98.4 11.7 %cholesky.147 = f32[128,128]{1,0:T(8,128)S(1)} custom-call(f32[128,128]{1,0:T(8,128)S(1)} %convolution_subtract_fusion.9), custom_call_target="Cholesky" | custom-call | tf_op jit(solution)/shard_map/jit(cholesky)/cholesky | solution.py:43
  116.1 19.9 %custom-call.18 = f32[2,128,128]{1,2,0:T(8,128)S(1)} custom-call(f32[2,128,128]{2,1,0:T(8,128)S(1)} %get-tuple-element.145), custom_call_target="InvertDiagBlocksLowerTriangular" | custom-call | tf_op jit(solution)/shard_map/triangular_solve/custom-call.0 | solution.py:44
  150.9 14.2 %fusion.3 = f32[4096,256]{0,1:T(8,128)} fusion(f32[4096,256]{0,1:T(8,128)S(1)} %bitcast.123, f32[4096,128]{0,1:T(8,128)S(1)} %fusion.45, f32[4096,128]{0,1:T(8,128)S(1)} %bitcast.121, pred[4096]{0:T(1024)(128)(4,1)S(1)} %get-tuple-element.199, pred[]{:T(512)S(6)} %eq.41, pred[4096]{0:T(1024)(128)(4,1)S(1)} %get-tuple-element.200), kind=kLoop, calls=%fused_computation.14 | loop fusion | flops 4194304 | bytes 12591105 | tf_op jit(solution)/shard_map/jit(_where)/select_n | solution.py:11
  169.4 86.1 %all-reduce.20.cloned.1.call-done = (f32[4096,256]{0,1:T(8,128)}, f32[256,256]{0,1:T(8,128)}) async-done(((f32[4096,256]{0,1:T(8,128)}, f32[256,256]{0,1:T(8,128)}), (f32[4096,256]{0,1:T(8,128)}, f32[256,256]{0,1:T(8,128)})) %all-reduce.20.cloned.1.call-update) | async-done | bytes 4456464 | tf_op jit(solution)/shard_map/psum | solution.py:11
  257.9 6.6 reshape.312
  267.1 152.7 %all-reduce.12.cloned.1.call-done = f32[8,2,256,256]{2,1,0,3:T(2,128)} async-done(((f32[8,2,256,256]{2,1,0,3:T(2,128)}), f32[8,2,256,256]{2,1,0,3:T(2,128)}) %all-reduce.12.cloned.1.call-update) | async-done | bytes 4194320 | tf_op jit(solution)/shard_map/psum | solution.py:11
  419.8 8.2 dynamic-slice_reduce_fusion.1
  430.2 33.4 %convolution_subtract_fusion.1 = f32[4096,2048]{0,1:T(8,128)} fusion(f32[4096,2048]{0,1:T(8,128)} %copy.20, f32[4096,256]{0,1:T(8,128)S(1)} %copy-done, pred[4096]{0:T(1024)(128)(4,1)S(1)} %get-tuple-element.200, f32[2048,256]{0,1:T(8,128)S(1)} %bitcast.116, pred[2048]{0:T(1024)(128)(4,1)S(1)} %fusion.66), kind=kOutput, calls=%fused_computation.5 | convolution fusion | flops 25779765248 | bytes 73406464 | tf_op jit(solution)/shard_map/dot_general | solution.py:67
  481.8 24.1 %all-reduce.14.cloned.1.call-done = f32[256,256]{0,1:T(8,128)} async-done(((f32[256,256]{0,1:T(8,128)}), f32[256,256]{0,1:T(8,128)}) %all-reduce.14.cloned.1.call-update) | async-done | bytes 262160 | tf_op jit(solution)/shard_map/psum | solution.py:11
  508.0 11.7 %cholesky.164 = f32[128,128]{1,0:T(8,128)S(1)} custom-call(f32[128,128]{1,0:T(8,128)S(1)} %cholesky.197), custom_call_target="Cholesky" | custom-call | tf_op jit(solution)/shard_map/jit(cholesky)/cholesky | solution.py:43
  519.8 9.8 %custom-call.19 = f32[1,128,128]{1,2,0:T(8,128)S(1)} custom-call(f32[1,128,128]{2,1,0:T(8,128)S(1)} %get-tuple-element.188), custom_call_target="InvertDiagBlocksLowerTriangular" | custom-call | tf_op jit(solution)/shard_map/jit(cholesky)/cholesky | solution.py:43
  530.1 11.9 %cholesky.181 = f32[128,128]{1,0:T(8,128)S(1)} custom-call(f32[128,128]{1,0:T(8,128)S(1)} %convolution_subtract_fusion.8), custom_call_target="Cholesky" | custom-call | tf_op jit(solution)/shard_map/jit(cholesky)/cholesky | solution.py:43
  554.7 19.7 %custom-call.20 = f32[2,128,128]{1,2,0:T(8,128)S(1)} custom-call(f32[2,128,128]{2,1,0:T(8,128)S(1)} %get-tuple-element.146), custom_call_target="InvertDiagBlocksLowerTriangular" | custom-call | tf_op jit(solution)/shard_map/triangular_solve/custom-call.0 | solution.py:44
  588.2 86.8 %all-reduce.18.cloned.1.call-done = (f32[4096,256]{0,1:T(8,128)}, f32[256,256]{0,1:T(8,128)}) async-done(((f32[4096,256]{0,1:T(8,128)}, f32[256,256]{0,1:T(8,128)}), (f32[4096,256]{0,1:T(8,128)}, f32[256,256]{0,1:T(8,128)})) %all-reduce.18.cloned.1.call-update) | async-done | bytes 4456464 | tf_op jit(solution)/shard_map/psum | solution.py:11
  677.5 6.8 reshape.314
  684.3 155.3 %all-reduce.16.cloned.1.call-done = f32[8,2,256,256]{2,1,0,3:T(2,128)} async-done(((f32[8,2,256,256]{2,1,0,3:T(2,128)}), f32[8,2,256,256]{2,1,0,3:T(2,128)}) %all-reduce.16.cloned.1.call-update) | async-done | bytes 4194320 | tf_op jit(solution)/shard_map/psum | solution.py:11
  839.6 8.2 dynamic-slice_reduce_fusion
  850.0 33.5 %convolution_subtract_fusion = f32[4096,2048]{0,1:T(8,128)} fusion(f32[4096,2048]{0,1:T(8,128)} %get-tuple-element.177, f32[4096,256]{0,1:T(8,128)S(1)} %copy-done.1, pred[4096]{0:T(1024)(128)(4,1)S(1)} %get-tuple-element.198, f32[2048,256]{0,1:T(8,128)S(1)} %bitcast.118, pred[2048]{0:T(1024)(128)(4,1)S(1)} %fusion.65), kind=kOutput, calls=%fused_computation.4 | convolution fusion | flops 25779765248 | bytes 73406464 | tf_op jit(solution)/shard_map/dot_general | solution.py:67
  891.8 33.4 %copy.29 = f32[4096,2048]{1,0:T(8,128)} copy(f32[4096,2048]{0,1:T(8,128)} %fusion.8) | data formatting | bytes 67108864
  925.2 6.4 convolution_subtract_fusion.4
  (111 shorter events, 114.8 us)
Async XLA Ops:
  7.2 67.1 %all-reduce.10.cloned.1.call-start = ((), (), s32[]{:S(2)}) async-start(), calls=%async_computation.1 | async-start | bytes 524288 | tf_op jit(solution)/shard_map/psum | solution.py:11
  7.2 32.9 %copy-start.3 = (f32[32,16384]{1,0:T(8,128)S(1)}, f32[32,16384]{1,0:T(8,128)}, u32[]{:S(2)}) copy-start(f32[32,16384]{1,0:T(8,128)} %param.28) | copy-start | bytes 6291460
  42.8 122.3 %all-to-all-start = ((f32[32,8,8,256]{3,1,0,2:T(8,128)}), f32[32,8,8,256]{3,1,0,2:T(8,128)}, u32[]{:S(2)}, u32[]{:S(2)}) async-start(f32[32,8,8,256]{3,1,0,2:T(8,128)} %copy.25), calls=%async_computation | async-start | bytes 4194304 | tf_op jit(solution)/shard_map/all_to_all | solution.py:28
  47.8 207.7 %all-reduce.20.cloned.1.call-start = ((), (), s32[]{:S(2)}) async-start(), calls=%async_computation.6 | async-start | bytes 8912896 | tf_op jit(solution)/shard_map/psum | solution.py:11
  169.3 250.5 %all-reduce.12.cloned.1.call-start = ((), (), s32[]{:S(2)}) async-start(), calls=%async_computation.2 | async-start | bytes 8388608 | tf_op jit(solution)/shard_map/psum | solution.py:11
  264.5 241.4 %all-reduce.14.cloned.1.call-start = ((), (), s32[]{:S(2)}) async-start(), calls=%async_computation.3 | async-start | bytes 524288 | tf_op jit(solution)/shard_map/psum | solution.py:11
  428.0 2.2 copy-start
  469.2 4.0 copy-start.4
  472.7 202.4 %all-reduce.18.cloned.1.call-start = ((), (), s32[]{:S(2)}) async-start(), calls=%async_computation.5 | async-start | bytes 8912896 | tf_op jit(solution)/shard_map/psum | solution.py:11
  581.5 3.7 copy-start.2
  588.2 251.4 %all-reduce.16.cloned.1.call-start = ((), (), s32[]{:S(2)}) async-start(), calls=%async_computation.4 | async-start | bytes 8388608 | tf_op jit(solution)/shard_map/psum | solution.py:11
  847.8 2.2 copy-start.1
  891.8 33.4 %copy-start.5 = (f32[256,256]{0,1:T(8,128)S(1)}, f32[256,256]{0,1:T(8,128)}, u32[]{:S(2)}) copy-start(f32[256,256]{0,1:T(8,128)} %get-tuple-element.170) | copy-start | bytes 786436
Sparse Core Ops, SparseCore 0:
  40.3 33.9 all-reduce.9
  169.5 85.9 all-reduce.19
  264.6 155.1 all-reduce.11
  472.8 33.0 all-reduce.13
  588.3 86.7 all-reduce.17
  684.4 155.1 all-reduce.15
where the time goes:
time: 960 us; the launch traced here: 944 us
  waiting for transfers between devices  531 us (55%)
  other arithmetic  158 us (16%)
  local copies, waits for them, and re-layouts  129 us (13%)
  matrix products  102 us (11%)
  between operations  17.5 us (2%)
    psum x6, waiting for transfers between devices, from_root(): return lax.psum(jnp.where(mine, shard, jnp.zeros_like(shard)), axis)  531 us
    unnamed x21, local copies, waits for them, and re-layouts  84.5 us
    another operation x13, other arithmetic, factorize(): factor = jnp.linalg.cholesky(corner)  68.8 us
    dot_general x2, matrix products, update(): lax.dot_general(left_part, right_part, contract, precision=exact, preferr...  66.9 us
    another operation x5, other arithmetic, factorize(): lax.linalg.triangular_solve(factor, slab, left_side=False, lower=True, tr...  39.7 us
    select_n x8, other arithmetic, from_root(): return lax.psum(jnp.where(mine, shard, jnp.zeros_like(shard)), axis)  25.9 us
    another operation x6, matrix products, factorize(): lax.linalg.triangular_solve(factor, slab, left_side=False, lower=True, tr...  19.7 us
  transfers between devices with their start and end apart: 7, of which 6 were waited for; matrix products, arithmetic and copies ran while one was open for 11% of the time, Pallas kernels for 0%

commit v1 on v0

v1 whole, which is shorter than its diff:
```python
import functools

import jax
import jax.numpy as jnp
from jax import lax
from jax.experimental import pallas as pl
from jax.experimental.pallas import tpu as pltpu
from jax.sharding import PartitionSpec as P

B = 256
K2 = 2 * B
H = 128
MESH = pl.DeviceIdType.MESH
EXACT = lax.Precision.HIGHEST


def exact_dot(a, b, dims):
    return lax.dot_general(a, b, (dims, ((), ())), precision=EXACT, preferred_element_type=jnp.float32)


def eliminate(t, carry, g_ref):
    g = g_ref[...]
    row = g_ref[pl.ds(t, 1), :]
    lane = lax.broadcasted_iota(jnp.int32, (H, H), 1)
    sub = lax.broadcasted_iota(jnp.int32, (H, 1), 0)
    lane_row = lax.broadcasted_iota(jnp.int32, (1, H), 1)
    col = jnp.sum(jnp.where(lane == t, g[:, :H], 0.0), axis=1, keepdims=True)
    pivot = jnp.sum(jnp.where(lane_row == t, row[:, :H], 0.0), axis=1, keepdims=True)
    scaled = row * (1.0 / pivot)
    g_ref[...] = g - jnp.where(sub > t, col, 0.0) * scaled
    return carry


def factor_step(step, w_ref, e_ref, g_ref):
    j = step // 2
    half = step % 2
    at = pl.multiple_of(j * H, H)
    eye = lax.broadcasted_iota(jnp.int32, (H, H), 0) == lax.broadcasted_iota(jnp.int32, (H, H), 1)

    @pl.when(half == 0)
    def _():
        g_ref[:, :H] = w_ref[pl.ds(at, H), pl.ds(at, H)]
        g_ref[:, H:] = jnp.where(eye, 1.0, 0.0)

    lax.fori_loop(half * (H // 2), half * (H // 2) + H // 2, functools.partial(eliminate, g_ref=g_ref), 0)

    @pl.when(half == 1)
    def _():
        g = g_ref[...]
        diag = jnp.sum(jnp.where(eye, g[:, :H], 0.0), axis=1, keepdims=True)
        inv = g[:, H:] * (1.0 / jnp.sqrt(diag))
        rw = exact_dot(inv, w_ref[pl.ds(at, H), :], ((1,), (0,)))
        re = exact_dot(inv, e_ref[pl.ds(at, H), :], ((1,), (0,)))
        lane = lax.broadcasted_iota(jnp.int32, (H, K2), 1)
        rm = jnp.transpose(jnp.where(lane >= (j + 1) * H, rw, 0.0))
        w_ref[...] -= exact_dot(rm, rw, ((1,), (0,)))
        e_ref[...] -= exact_dot(rm, re, ((1,), (0,)))
        e_ref[pl.ds(at, H), :] = re


def exchange(
    R, C, tr, cross, pan, q, linv, ans, tq,
    w_ref, g_ref, zs, zb, zr, ps, pr, ss, sr, loc, xs, xr, ts, trv,
):
    m, n = tr.shape
    fq = cross.shape[0]
    nb = n // B
    npl = 1 + m // K2
    N = C // 2
    r = lax.axis_index("row")
    c = lax.axis_index("col")
    k = c % 2
    chip = c // 2
    y = chip // 2
    p = jnp.where(chip % 2 == 0, (N - y) % N, y + 1)

    def chip_at(pos):
        return jnp.where(pos > N // 2, 2 * (N - pos), jnp.maximum(2 * pos - 1, 0))

    nxt = [2 * chip_at((p + 1) % N) + k, 2 * chip_at((p + N - 1) % N) + k]
    last = [p == N - 1, p == 1]
    sib = c + 1 - 2 * k
    half_rows = m // 2

    own_q = [pltpu.make_async_copy(tr.at[pl.ds(0, B), :], q.at[pl.ds(t * B, B), :], loc.at[t]) for t in range(2)]
    own_p = [
        pltpu.make_async_copy(
            tr.at[pl.ds(d * half_rows, half_rows), pl.ds(0, B)],
            pan.at[k, d, pl.ds(B, half_rows), :],
            loc.at[2 + d],
        )
        for d in range(2)
    ]
    own_t = pltpu.make_async_copy(cross.at[:, pl.ds(0, K2)], tq.at[pl.ds(c * fq, fq), :], loc.at[4])

    def own_x(b):
        src = pl.multiple_of((b * C + c) * B, B)
        return pltpu.make_async_copy(
            cross.at[:, pl.ds(src, B)], ans.at[pl.ds(c * fq, fq), pl.ds(b * B, B)], loc.at[5 + b]
        )

    for t in range(2):
        @pl.when(r == t)
        def _():
            own_q[t].start()

        @pl.when(p == 0)
        def _():
            own_p[t].start()

    own_t.start()
    for b in range(nb):
        own_x(b).start()

    barrier = pltpu.get_barrier_semaphore()
    for o in range(1, C):
        pl.semaphore_signal(barrier, inc=1, device_id=(r, (c + o) % C), device_id_type=MESH)

    for o in (1, R - 1):
        pl.semaphore_signal(barrier, inc=1, device_id=((r + o) % R, c), device_id_type=MESH)
    pl.semaphore_wait(barrier, C + 1)

    for t in range(2):
        @pl.when(r == t)
        def _():
            own_q[t].wait()

        @pl.when(p == 0)
        def _():
            own_p[t].wait()

    def z_copy(t, b, down):
        piece = q.at[pl.ds(t * B, B), pl.ds(pl.multiple_of(b * B, B), B)]
        to = jnp.maximum(r - 1, 0) if down else jnp.minimum(r + 1, R - 1)
        return pltpu.make_async_remote_copy(
            piece, piece, zb.at[b] if down else zs.at[t, b], zr.at[t, b], device_id=(to, c), device_id_type=MESH
        )

    def p_copy(d, i):
        piece = pan.at[k, d, pl.ds(pl.multiple_of(i * B, B), B), :]
        return pltpu.make_async_remote_copy(
            piece, piece, ps.at[d, i], pr.at[d, i], device_id=(r, nxt[d]), device_id_type=MESH
        )

    def s_copy(d, i, core):
        piece = pan.at[core, d, pl.ds(pl.multiple_of(i * B, B), B), :]
        return pltpu.make_async_remote_copy(
            piece, piece, ss.at[d, i], sr.at[d, i], device_id=(r, sib), device_id_type=MESH
        )

    def x_copy(o, b):
        peer = (c + o) % C
        src = pl.multiple_of((b * C + peer) * B, B)
        return pltpu.make_async_remote_copy(
            cross.at[:, pl.ds(src, B)],
            ans.at[pl.ds(c * fq, fq), pl.ds(pl.multiple_of(b * B, B), B)],
            xs.at[o, b], xr.at[o, b], device_id=(r, peer), device_id_type=MESH,
        )

    def t_copy(o):
        return pltpu.make_async_remote_copy(
            cross.at[:, pl.ds(0, K2)], tq.at[pl.ds(c * fq, fq), :],
            ts.at[o], trv.at[o], device_id=(r, (c + o) % C), device_id_type=MESH,
        )

    def guarded(i, count, work):
        @pl.when(jnp.logical_and(i >= 0, i < count))
        def _():
            work(i)

    def z_pass(t, i):
        z_copy(t, i, False).wait_recv()

        @pl.when(jnp.logical_and(r > t, r < R - 1))
        def _():
            z_copy(t, i, False).start()

    def z_send(b, carry):
        for t in range(2):
            @pl.when(r == t)
            def _():
                z_copy(t, b, False).start()

        @pl.when(r == 1)
        def _():
            z_copy(1, b, True).start()

        return carry

    def z_item(step):
        for t in range(2):
            @pl.when(r != t)
            def _():
                lag = jnp.where(r > t, r - t - 1, 0)
                guarded(step - lag - 1, nb - 1, lambda i, t=t: z_pass(t, i + 1))

    def p_pass(d, i):
        @pl.when(p != 0)
        def _():
            p_copy(d, i).wait_recv()

            @pl.when(jnp.logical_not(last[d]))
            def _():
                p_copy(d, i).start()

        s_copy(d, i, k).start()

    def p_item(step):
        for d in range(2):
            hops = p if d == 0 else N - p
            lag = jnp.where(p == 0, 0, hops - 1)
            i = step - lag
            guarded(i - 1, npl - 1, lambda i, d=d: p_pass(d, i + 1))

    lax.fori_loop(0, nb, z_send, 0)
    for t in range(2):
        @pl.when(r != t)
        def _():
            z_pass(t, 0)

    @pl.when(p == 0)
    def _():
        for d in range(2):
            pltpu.make_async_copy(
                q.at[pl.ds(d * B, B), pl.ds(0, B)], pan.at[k, d, pl.ds(0, B), :], loc.at[d]
            ).start()
        for d in range(2):
            pltpu.make_async_copy(
                q.at[pl.ds(d * B, B), pl.ds(0, B)], pan.at[k, d, pl.ds(0, B), :], loc.at[d]
            ).wait()

    @pl.when(p == 0)
    def _():
        for d in range(2):
            p_copy(d, 0).start()

        def p_send(i, carry):
            for d in range(2):
                p_copy(d, i).start()
            return carry

        lax.fori_loop(1, npl, p_send, 0)

    def first(d):
        p_pass(d, 0)

    @pl.when(p <= N // 2)
    def _():
        first(0)
        first(1)

    @pl.when(p > N // 2)
    def _():
        first(1)
        first(0)

    for o in range(1, C):
        t_copy(o).start()
    for d in range(2):
        s_copy(d, 0, 1 - k).wait_recv()
    loads = [
        pltpu.make_async_copy(
            pan.at[core, d, pl.ds(0, B), :], w_ref.at[pl.ds(d * B, B), pl.ds(core * B, B)], loc.at[2 * core + d]
        )
        for core in range(2)
        for d in range(2)
    ]
    for load in loads:
        load.start()
    own_sub = lax.broadcasted_iota(jnp.int32, (K2, K2), 0)
    own_lane = lax.broadcasted_iota(jnp.int32, (K2, K2), 1)
    linv[...] = jnp.where(own_sub == own_lane, 1.0, 0.0)
    for load in loads:
        load.wait()

    steps = 2 * (K2 // H)

    def body(s, carry):
        z_item(s)
        p_item(s)

        @pl.when(s <= nb)
        def _():
            for o in range(1, C):
                x_copy(o, s - 1).start()

        @pl.when(s <= steps)
        def _():
            factor_step(s - 1, w_ref, linv, g_ref)

        return carry

    lax.fori_loop(1, max(nb + R, npl + N, steps) + 1, body, 0)

    own_t.wait()
    for b in range(nb):
        own_x(b).wait()

    def drain_z(b, carry):
        for t in range(2):
            @pl.when(jnp.logical_and(r >= t, r < R - 1))
            def _():
                z_copy(t, b, False).wait_send()

        @pl.when(r == 1)
        def _():
            z_copy(1, b, True).wait_send()

        for o in range(1, C):
            x_copy(o, b).wait_send()
            peer = (c + C - o) % C
            pltpu.make_async_remote_copy(
                cross.at[:, pl.ds(0, B)],
                ans.at[pl.ds(peer * fq, fq), pl.ds(pl.multiple_of(b * B, B), B)],
                xs.at[o, b], xr.at[o, b], device_id=(r, peer), device_id_type=MESH,
            ).wait_recv()
        return carry

    lax.fori_loop(0, nb, drain_z, 0)

    def drain_p(i, carry):
        for d in range(2):
            @pl.when(jnp.logical_not(last[d]))
            def _():
                p_copy(d, i).wait_send()

            s_copy(d, i, k).wait_send()

            @pl.when(i > 0)
            def _():
                s_copy(d, i, 1 - k).wait_recv()
        return carry

    lax.fori_loop(0, npl, drain_p, 0)
    for o in range(1, C):
        t_copy(o).wait_send()
        peer = (c + C - o) % C
        pltpu.make_async_remote_copy(
            cross.at[:, pl.ds(0, K2)], tq.at[pl.ds(peer * fq, fq), :],
            ts.at[o], trv.at[o], device_id=(r, peer), device_id_type=MESH,
        ).wait_recv()


def split(x):
    hi = x.astype(jnp.bfloat16)
    return hi, (x - hi.astype(jnp.float32)).astype(jnp.bfloat16)


def solve_rows(x0, x1, linv):
    c0 = exact_dot(x0, linv[:B, :B], ((1,), (1,)))
    c1 = exact_dot(x0, linv[B:, :B], ((1,), (1,))) + exact_dot(x1, linv[B:, B:], ((1,), (1,)))
    return c0, c1


def update(R, C, pan, q, linv, tr, ans, tq, out, sol, hi_ref, lo_ref):
    i = pl.program_id(0)
    r = lax.axis_index("row")
    c = lax.axis_index("col")
    n = q.shape[1]
    width = min(n, 512)

    def product(hi, lo, cols):
        dot = functools.partial(jnp.dot, preferred_element_type=jnp.float32)
        mh = hi_ref[:, cols]
        return dot(hi, mh) + dot(hi, lo_ref[:, cols]) + dot(lo, mh)

    @pl.when(i == 0)
    def _():
        for a in range(0, n, width):
            cols = slice(a, a + width)
            q0 = q[:B, cols]
            m0 = exact_dot(linv[:B, :B], q0, ((1,), (0,)))
            m1 = exact_dot(linv[B:, :B], q0, ((1,), (0,))) + exact_dot(linv[B:, B:], q[B:, cols], ((1,), (0,)))
            hi_ref[:B, cols], lo_ref[:B, cols] = split(m0)
            hi_ref[B:, cols], lo_ref[B:, cols] = split(m1)
        y0, y1 = solve_rows(tq[:, :B], tq[:, B:], linv)
        hi, lo = split(jnp.concatenate([y0, y1], axis=1))
        for a in range(0, n, width):
            cols = slice(a, a + width)
            sol[:, cols] = ans[:, cols] - product(hi, lo, cols)

        @pl.when(c == 0)
        def _():
            sol[:, :B] = y0

        @pl.when(c == 1)
        def _():
            sol[:, :B] = y1

    tile = i * R + r
    c0, c1 = solve_rows(pan[0, 0], pan[1, 0], linv)
    low = lax.broadcasted_iota(jnp.int32, (B, B), 0) >= lax.broadcasted_iota(jnp.int32, (B, B), 1)
    c0 = jnp.where(jnp.logical_or(tile > 0, low), c0, 0.0)
    c1 = jnp.where(jnp.logical_or(tile > 1, jnp.logical_and(low, tile == 1)), c1, 0.0)

    @pl.when(tile <= 1)
    def _():
        out[...] = jnp.zeros_like(out)

    @pl.when(tile > 1)
    def _():
        hi, lo = split(jnp.concatenate([c0, c1], axis=1))
        for a in range(0, n, width):
            cols = slice(a, a + width)
            out[:, cols] = tr[:, cols] - product(hi, lo, cols)

    @pl.when(c == 0)
    def _():
        out[:, :B] = c0

    @pl.when(c == 1)
    def _():
        out[:, :B] = c1


def on_device(R, C, trailing, cross):
    m, n = trailing.shape
    fq = cross.shape[0]
    nb = n // B
    h = m // K2
    npl = 1 + h
    f32 = jnp.float32
    anywhere = pl.BlockSpec(memory_space=pl.ANY)
    vmem = pl.BlockSpec(memory_space=pltpu.VMEM)
    dma = pltpu.SemaphoreType.DMA
    pan, q, linv, ans, tq = pl.pallas_call(
        functools.partial(exchange, R, C),
        out_shape=(
            jax.ShapeDtypeStruct((2, 2, B + m // 2, B), f32),
            jax.ShapeDtypeStruct((K2, n), f32),
            jax.ShapeDtypeStruct((K2, K2), f32),
            jax.ShapeDtypeStruct((fq * C, n), f32),
            jax.ShapeDtypeStruct((fq * C, K2), f32),
        ),
        in_specs=[anywhere, anywhere],
        out_specs=(anywhere, anywhere, vmem, anywhere, anywhere),
        scratch_shapes=[
            pltpu.VMEM((K2, K2), f32),
            pltpu.VMEM((H, 2 * H), f32),
            dma((2, nb)), dma((nb,)), dma((2, nb)),
            dma((2, npl)), dma((2, npl)), dma((2, npl)), dma((2, npl)),
            dma((5 + nb,)),
            dma((C, nb)), dma((C, nb)), dma((C,)), dma((C,)),
        ],
        compiler_params=pltpu.CompilerParams(
            collective_id=0, has_side_effects=True, vmem_limit_bytes=32 * 1024 * 1024
        ),
        cost_estimate=pl.CostEstimate(flops=10**9, bytes_accessed=32 * 10**6, transcendentals=0),
        name="exchange",
    )(trailing, cross)

    def whole(shape):
        return pl.BlockSpec(shape, lambda i: (0,) * len(shape))

    return pl.pallas_call(
        functools.partial(update, R, C),
        grid=(m // B,),
        out_shape=(jax.ShapeDtypeStruct((m, n), f32), jax.ShapeDtypeStruct((fq * C, n), f32)),
        in_specs=[
            pl.BlockSpec((2, 1, B, B), lambda i: (0, i // h, 1 + i % h, 0)),
            whole((K2, n)),
            whole((K2, K2)),
            pl.BlockSpec((B, n), lambda i: (i, 0)),
            whole((fq * C, n)),
            whole((fq * C, K2)),
        ],
        out_specs=(pl.BlockSpec((B, n), lambda i: (i, 0)), whole((fq * C, n))),
        scratch_shapes=[pltpu.VMEM((K2, n), jnp.bfloat16), pltpu.VMEM((K2, n), jnp.bfloat16)],
        compiler_params=pltpu.CompilerParams(
            dimension_semantics=("arbitrary",), vmem_limit_bytes=52 * 1024 * 1024
        ),
        cost_estimate=pl.CostEstimate(flops=2 * m * n * K2 * 3, bytes_accessed=8 * m * n, transcendentals=0),
        name="update",
    )(pan, q, linv, trailing, ans, tq)


def solution(mesh):
    return jax.shard_map(
        functools.partial(on_device, mesh.shape["row"], mesh.shape["col"]),
        mesh=mesh,
        in_specs=(P("row", "col"), P(("row", "col"), None)),
        out_specs=(P("row", "col"), P("row", "col")),
        check_vma=False,
    )
```

time: 960 us -> 244 us (0.25); the launches traced: 944 us -> 244 us
  waiting for transfers between devices: 531 us -> 0 us
  Pallas kernels: 0 us -> 234 us
  other arithmetic: 158 us -> 0 us
  local copies, waits for them, and re-layouts: 129 us -> 8.56 us
  matrix products: 102 us -> 0 us
  between operations: 17.5 us -> 0.66 us
    psum x6 -> x0, waiting for transfers between devices: 531 us -> none  [from_root(): return lax.psum(jnp.where(mine, shard, jnp.zeros_like(shard)), axis)]
    pallas_call x0 -> x2, Pallas kernels: none -> 234 us  [the longest x1 177 us: on_device(): pl.pallas_call(functools.partial(exchange, R, C), out_shape=(jax.ShapeDty...]
    another operation x19 -> x0, other arithmetic: 109 us -> none  [the longest x13 68.8 us: factorize(): factor = jnp.linalg.cholesky(corner)]
    dot_general x4 -> x0, matrix products: 79.7 us -> none  [the longest x2 66.9 us: update(): lax.dot_general(left_part, right_part, contract, precision=exact, preferr...]
    unnamed x21 -> x8, local copies, waits for them, and re-layouts: 84.5 us -> 8.56 us
    select_n x8 -> x0, other arithmetic: 25.9 us -> none  [from_root(): return lax.psum(jnp.where(mine, shard, jnp.zeros_like(shard)), axis)]
    another operation x16 -> x0, matrix products: 22.5 us -> none  [the longest x6 19.7 us: factorize(): lax.linalg.triangular_solve(factor, slab, left_side=False, lower=True, tr...]
    scatter x6 -> x0, other arithmetic: 21.2 us -> none  [the longest x2 11 us: finish(): state.at[:, col_block * B:(col_block + 1) * B]]
  transfers between devices with their start and end apart: 7 -> 0, of which waited for: 6 -> 0; matrix products, arithmetic and copies ran while one was open for 11% -> 0% of each run, Pallas kernels for 0% -> 0%
where the time goes in v1:
time: 244 us
  Pallas kernels  234 us (96%)
  local copies, waits for them, and re-layouts  8.56 us (4%)
    pallas_call x1, Pallas kernels, on_device(): pl.pallas_call(functools.partial(exchange, R, C), out_shape=(jax.ShapeDty...  177 us
    pallas_call x1, Pallas kernels, on_device(): pl.pallas_call(functools.partial(update, R, C), grid=(m // B,), out_shape...  57.4 us
    unnamed x8, local copies, waits for them, and re-layouts  8.56 us

profile of v1, /device:TPU:29, one launch (start us, length us, event | category | flops | bytes accessed | tf_op | source)
XLA Modules:
  0.0 243.7 jit_solution(6769165166285646642)
XLA Ops:
  0.6 0.0 copy-start
  0.6 1.6 copy-done
  2.2 177.0 %exchange.1 = (f32[2,2,2304,256]{3,2,1,0:T(8,128)S(1)}, f32[512,2048]{1,0:T(8,128)S(1)}, f32[512,512]{1,0:T(8,128)S(1)}, f32[256,2048]{1,0:T(8,128)S(1)}, f32[256,512]{1,0:T(8,128)S(1)}) custom-call(f32[4096,2048]{1,0:T(8,128)} %tr.3, f32[32,16384]{1,0:T(8,128)S(1)} %copy-done), custom_call_target="tpu_custom_call" | custom-call | flops 1000000000 | bytes 32000000 | tf_op jit(solution)/shard_map/exchange/pallas_call | solution.py:426
  179.2 0.0 copy-start.1
  179.2 3.6 %copy-done.1 = f32[2,2,2304,256]{3,2,1,0:T(8,128)} copy-done((f32[2,2,2304,256]{3,2,1,0:T(8,128)}, f32[2,2,2304,256]{3,2,1,0:T(8,128)S(1)}, u32[]{:S(2)}) %copy-start.1) | copy-done | bytes 9437208
  182.9 0.0 copy-start.2
  182.9 2.1 copy-done.2
  184.9 0.0 copy-start.3
  184.9 1.3 copy-done.3
  186.2 57.4 %update.1 = (f32[4096,2048]{1,0:T(8,128)}, f32[256,2048]{1,0:T(8,128)}) custom-call(f32[2,2,2304,256]{3,2,1,0:T(8,128)} %copy-done.1, f32[512,2048]{1,0:T(8,128)} %copy-done.2, f32[512,512]{1,0:T(8,128)S(1)} %get-tuple-element.9.linv, f32[4096,2048]{1,0:T(8,128)} %tr.3, f32[256,2048]{1,0:T(8,128)} %copy-done.3, f32[256,512]{1,0:T(8,128)S(1)} %get-tuple-element.11.tq), custom_call_target="tpu_custom_call" | custom-call | flops 25769803776 | bytes 67108864 | tf_op jit(solution)/shard_map/update/pallas_call | solution.py:455
Async XLA Ops:
  0.6 1.6 copy-start
  179.2 3.6 %copy-start.1 = (f32[2,2,2304,256]{3,2,1,0:T(8,128)}, f32[2,2,2304,256]{3,2,1,0:T(8,128)S(1)}, u32[]{:S(2)}) copy-start(f32[2,2,2304,256]{3,2,1,0:T(8,128)S(1)} %get-tuple-element.7.pan) | copy-start | bytes 28311556
  182.9 2.1 copy-start.2
  184.9 1.3 copy-start.3
